TPU v7x, 512 devices: a whole 4x4x16 slice. The times are simulated.
512 devices in a mesh: seq: 8 (over z_hi, core), ffn: 64 (over x, z_lo, y).
Axes of the slice: x: 4, y: 4, z: 16 (z_hi: 4, z_lo: 4; z = z_hi * 4 + z_lo), core: 2. Of those that a mesh axis runs over, the one named last changes fastest.
Arguments:
- teacher_rows: bfloat16 [1024, 4096], P('ffn', 'seq'), may hold values from -6 to 6
- grad_out: bfloat16 [1024, 4096], P('ffn', 'seq'), may hold values from -0.1875 to 0.1875
- w_gate: bfloat16 [4096, 16384], P('seq', 'ffn'), may hold values from -0.125 to 0.125
- w_up: bfloat16 [4096, 16384], P('seq', 'ffn'), may hold values from -0.125 to 0.125
- w_down: bfloat16 [16384, 4096], P('ffn', 'seq'), may hold values from -0.0625 to 0.0625
- mask_gate: int32 [32, 128], P('seq', 'ffn'), may hold values from 0 to 1, as said below
- mask_up: int32 [32, 128], P('seq', 'ffn'), may hold values from 0 to 1, as said below
- mask_down: int32 [128, 32], P('ffn', 'seq'), may hold values from 0 to 1, as said below
Outputs:
- layer_out: bfloat16 [1024, 4096], P('ffn', 'seq')
- grad_gate: float32 [4096, 16384], P('seq', 'ffn')
- grad_up: float32 [4096, 16384], P('seq', 'ffn')
- grad_down: float32 [16384, 4096], P('ffn', 'seq')
Inputs may be any that keep to these rules, and one draw needn't show every extreme that they name: `mask_gate`: each block is kept (1) or dropped (0); the share of kept blocks differs from one column of blocks to another. `mask_up`: each block is kept (1) or dropped (0); the share of kept blocks differs from one column of blocks to another. `mask_down`: each block is kept (1) or dropped (0); the share of kept blocks differs from one row of blocks to another.
All inputs are finite; a program needn't handle non-finite values.
Results may differ from a plain program's by a relative error of at most 0.027.
Values may be sent and summed in bfloat16 or wider, within the bound.
A program may use at most 64 MiB of HBM per device.

v0:
```python
import jax
import jax.numpy as jnp
from jax import lax
from jax.sharding import PartitionSpec as P

BLK = 128


def keep_blocks(weight, block_mask):
    height, breadth = weight.shape
    tiles = weight.reshape(height // BLK, BLK, breadth // BLK, BLK)
    kept = tiles * block_mask.astype(weight.dtype)[:, None, :, None]
    return kept.reshape(height, breadth)


def inner_rows(left, right):
    return lax.dot_general(
        left, right, (((0,), (0,)), ((), ())), preferred_element_type=jnp.float32
    )


def inner_cols(left, right):
    return lax.dot_general(
        left, right, (((1,), (1,)), ((), ())), preferred_element_type=jnp.float32
    )


def activate(gate, up_sum):
    sigmoid = jax.nn.sigmoid(gate)
    active = gate * sigmoid
    return ((active * up_sum).astype(jnp.bfloat16), sigmoid, active)


def backprop(d_hidden, gate, up_sum, sigmoid, active):
    d_gate = (d_hidden * up_sum * sigmoid * (1.0 + gate * (1.0 - sigmoid))).astype(jnp.bfloat16)
    d_up = (d_hidden * active).astype(jnp.bfloat16)
    return (d_gate, d_up)


def on_device(teacher_rows, grad_out, w_gate, w_up, w_down, mask_gate, mask_up, mask_down):
    gate_kept = keep_blocks(w_gate, mask_gate)
    up_kept = keep_blocks(w_up, mask_up)
    down_kept = keep_blocks(w_down, mask_down)
    rows_all = lax.all_gather(teacher_rows, "ffn", axis=0, tiled=True)
    gate_part = jnp.dot(rows_all, gate_kept, preferred_element_type=jnp.float32)
    up_part = jnp.dot(rows_all, up_kept, preferred_element_type=jnp.float32)
    gate_own, up_own = (
        lax.psum_scatter(
            gate_part.astype(jnp.bfloat16), "seq", scatter_dimension=0, tiled=True
        ).astype(jnp.float32),
        lax.psum_scatter(
            up_part.astype(jnp.bfloat16), "seq", scatter_dimension=0, tiled=True
        ).astype(jnp.float32),
    )
    hidden_own, sigmoid, active = activate(gate_own, up_own)
    hidden_all = lax.all_gather(hidden_own, "seq", axis=0, tiled=True)
    layer_out = lax.psum_scatter(
        jnp.dot(hidden_all, down_kept, preferred_element_type=jnp.float32),
        "ffn",
        scatter_dimension=0,
        tiled=True,
    ).astype(jnp.bfloat16)
    grads_all = lax.all_gather(grad_out, "ffn", axis=0, tiled=True)
    hidden_part = inner_cols(grads_all, down_kept)
    grad_down = keep_blocks(inner_rows(hidden_all, grads_all), mask_down)
    d_hidden = lax.psum_scatter(
        hidden_part.astype(jnp.bfloat16), "seq", scatter_dimension=0, tiled=True
    ).astype(jnp.float32)
    d_gate_own, d_up_own = backprop(d_hidden, gate_own, up_own, sigmoid, active)
    d_gate_all, d_up_all = (
        lax.all_gather(d_gate_own, "seq", axis=0, tiled=True),
        lax.all_gather(d_up_own, "seq", axis=0, tiled=True),
    )
    grad_gate = keep_blocks(inner_rows(rows_all, d_gate_all), mask_gate)
    grad_up = keep_blocks(inner_rows(rows_all, d_up_all), mask_up)
    return (layer_out, grad_gate, grad_up, grad_down)


def solution(mesh):
    return jax.shard_map(
        on_device,
        mesh=mesh,
        in_specs=(
            P("ffn", "seq"),
            P("ffn", "seq"),
            P("seq", "ffn"),
            P("seq", "ffn"),
            P("ffn", "seq"),
            P("seq", "ffn"),
            P("seq", "ffn"),
            P("ffn", "seq"),
        ),
        out_specs=(P("ffn", "seq"), P("seq", "ffn"), P("seq", "ffn"), P("ffn", "seq")),
        check_vma=False,
    )
```

profile of v0, /device:TPU:128, one launch (start us, length us, event | category | flops | bytes accessed | tf_op | source)
XLA Modules:
  0.0 1291.6 jit_solution(10910990780994086637)
XLA Ops:
  7.2 0.0 all-gather.3.cloned.1.call-start
  7.2 0.7 all-gather.3.cloned.1.call-update
  7.9 0.0 all-gather.5.cloned.1.call-start
  8.0 0.7 all-gather.5.cloned.1.call-update
  8.7 0.0 reduce-scatter.13.cloned.1.call-start
  8.7 0.8 fusion.19
  9.5 0.1 copy.16
  9.6 355.3 %all-gather.3.cloned.1.call-done = bf16[1024,512]{1,0:T(8,128)(2,1)} async-done(((bf16[16,512]{1,0:T(8,128)(2,1)}), bf16[1024,512]{1,0:T(8,128)(2,1)}) %all-gather.3.cloned.1.call-update) | async-done | bytes 1048592 | tf_op jit(solution)/shard_map/all_gather | solution.py:44
  364.9 0.2 mul.87
  365.1 1.9 fusion
  367.0 1.0 copy.20
  368.0 0.0 reduce-scatter.13.cloned.1.call-update
  368.0 0.0 copy-start.5
  368.1 0.0 reduce-scatter.15.cloned.1.call-start
  368.1 0.1 copy.17
  368.2 0.2 mul.91
  368.5 0.5 fusion.1
  369.0 1.0 copy.22
  370.0 0.0 reduce-scatter.15.cloned.1.call-update
  370.0 0.0 reduce-scatter.17.cloned.1.call-start
  370.1 346.8 %all-gather.5.cloned.1.call-done = bf16[1024,512]{1,0:T(8,128)(2,1)} async-done(((bf16[16,512]{1,0:T(8,128)(2,1)}), bf16[1024,512]{1,0:T(8,128)(2,1)}) %all-gather.5.cloned.1.call-update) | async-done | bytes 1048592 | tf_op jit(solution)/shard_map/all_gather | solution.py:63
  716.8 0.1 mul.95
  717.0 1.7 fusion.2
  718.7 1.0 copy.24
  719.7 0.0 reduce-scatter.17.cloned.1.call-update
  719.7 0.0 reduce-scatter.11.cloned.1.call-start
  719.8 44.5 %reduce-scatter.13.cloned.1.call-done = bf16[128,256]{1,0:T(8,128)(2,1)} async-done(((bf16[1024,256]{1,0:T(8,128)(2,1)}), bf16[128,256]{1,0:T(8,128)(2,1)}) %reduce-scatter.13.cloned.1.call-update) | async-done | bytes 65552
  764.2 0.9 copy.21
  765.2 50.5 %reduce-scatter.15.cloned.1.call-done = bf16[128,256]{1,0:T(8,128)(2,1)} async-done(((bf16[1024,256]{1,0:T(8,128)(2,1)}), bf16[128,256]{1,0:T(8,128)(2,1)}) %reduce-scatter.15.cloned.1.call-update) | async-done | bytes 65552
  815.7 0.9 copy.23
  816.6 50.3 %reduce-scatter.17.cloned.1.call-done = bf16[128,256]{1,0:T(8,128)(2,1)} async-done(((bf16[1024,256]{1,0:T(8,128)(2,1)}), bf16[128,256]{1,0:T(8,128)(2,1)}) %reduce-scatter.17.cloned.1.call-update) | async-done | bytes 65552
  867.0 0.9 copy.25
  867.9 0.1 fusion.11
  868.0 32.7 %all_gather.16 = bf16[1024,256]{0,1:T(8,128)(2,1)S(1)} all-gather(bf16[128,256]{0,1:T(8,128)(2,1)S(1)} %get-tuple-element.14), channel_id=1, replica_groups=mesh['seq'=8,'ffn'=64] {'seq'}, dimensions={0}, use_global_device_ids=true | all-gather | bytes 589824 | tf_op jit(solution)/shard_map/all_gather | solution.py:56
  900.7 1.8 fusion.16
  902.5 0.0 reduce-scatter.11.cloned.1.call-update
  902.5 25.4 %all_gather.18 = bf16[1024,256]{0,1:T(8,128)(2,1)S(1)} all-gather(bf16[128,256]{0,1:T(8,128)(2,1)S(1)} %get-tuple-element.13), channel_id=1, replica_groups=mesh['seq'=8,'ffn'=64] {'seq'}, dimensions={0}, use_global_device_ids=true | all-gather | bytes 589824 | tf_op jit(solution)/shard_map/all_gather | solution.py:71
  928.0 0.1 mul.102
  928.1 0.4 fusion.4
  928.6 1.0 copy.18
  929.6 26.9 %all_gather.19 = bf16[1024,256]{0,1:T(8,128)(2,1)S(1)} all-gather(bf16[128,256]{0,1:T(8,128)(2,1)S(1)} %get-tuple-element.12), channel_id=1, replica_groups=mesh['seq'=8,'ffn'=64] {'seq'}, dimensions={0}, use_global_device_ids=true | all-gather | bytes 589824 | tf_op jit(solution)/shard_map/all_gather | solution.py:72
  956.5 0.1 mul.106
  956.7 0.4 fusion.3
  957.1 1.0 copy.19
  958.1 0.1 mul.109
  958.3 1.2 convolution_multiply_fusion
  959.5 323.9 %reduce-scatter.11.cloned.1.call-done = f32[16,512]{1,0:T(8,128)} async-done(((f32[1024,512]{1,0:T(8,128)}), f32[16,512]{1,0:T(8,128)}) %reduce-scatter.11.cloned.1.call-update) | async-done | bytes 32784 | tf_op jit(solution)/shard_map/reduce_scatter | solution.py:57
  1283.4 1.4 convert_element_type.67
  (13 shorter events, 0.0 us)
Async XLA Ops:
  7.2 360.9 %copy-start.4 = (s32[4,2]{0,1:T(2,128)S(1)}, s32[4,2]{0,1:T(2,128)}, u32[]{:S(2)}) copy-start(s32[4,2]{0,1:T(2,128)} %param.14) | copy-start | bytes 100
  7.2 357.7 %all-gather.3.cloned.1.call-start = ((), (), s32[]{:S(2)}) async-start(), calls=%async_computation.4 | async-start | bytes 1064960 | tf_op jit(solution)/shard_map/all_gather | solution.py:44
  7.9 708.9 %all-gather.5.cloned.1.call-start = ((), (), s32[]{:S(2)}) async-start(), calls=%async_computation.6 | async-start | bytes 1064960 | tf_op jit(solution)/shard_map/all_gather | solution.py:63
  8.7 755.6 %reduce-scatter.13.cloned.1.call-start = ((), (), s32[]{:S(2)}) async-start(), calls=%async_computation.7 | async-start | bytes 589824
  9.6 358.9 %copy-start.3 = (bf16[512,256]{1,0:T(8,128)(2,1)S(1)}, bf16[512,256]{1,0:T(8,128)(2,1)}, u32[]{:S(2)}) copy-start(bf16[512,256]{1,0:T(8,128)(2,1)} %param.11) | copy-start | bytes 786436
  364.9 3.6 copy-start
  368.0 2.0 copy-start.5
  368.1 447.6 %reduce-scatter.15.cloned.1.call-start = ((), (), s32[]{:S(2)}) async-start(), calls=%async_computation.8 | async-start | bytes 589824
  368.2 348.7 %copy-start.2 = (bf16[256,512]{1,0:T(8,128)(2,1)S(1)}, bf16[256,512]{1,0:T(8,128)(2,1)}, u32[]{:S(2)}) copy-start(bf16[256,512]{1,0:T(8,128)(2,1)} %param.12) | copy-start | bytes 786436
  370.0 497.0 %reduce-scatter.17.cloned.1.call-start = ((), (), s32[]{:S(2)}) async-start(), calls=%async_computation.9 | async-start | bytes 589824
  719.7 563.7 %reduce-scatter.11.cloned.1.call-start = ((), (), s32[]{:S(2)}) async-start(), calls=%async_computation.5 | async-start | bytes 2129920 | tf_op jit(solution)/shard_map/reduce_scatter | solution.py:57
  956.6 1.6 copy-start.1
Sparse Core Ops, SparseCore 0:
  10.1 354.7 all-gather.2
  367.0 349.7 all-gather.4
  720.2 43.9 reduce-scatter.12
  767.7 47.9 reduce-scatter.14
  818.9 48.0 reduce-scatter.16
  902.7 380.6 reduce-scatter.10
where the time goes:
time: 1290 us
  waiting for transfers between devices  1170 us (91%)
  blocking collectives  85.1 us (7%)
  between operations  14.3 us (1%)
    all_gather x1, waiting for transfers between devices, on_device(): rows_all = lax.all_gather(teacher_rows, 'ffn', axis=0, tiled=True)  355 us
    all_gather x1, waiting for transfers between devices, on_device(): grads_all = lax.all_gather(grad_out, 'ffn', axis=0, tiled=True)  347 us
    reduce_scatter x1, waiting for transfers between devices, on_device(): lax.psum_scatter(jnp.dot(hidden_all, down_kept, preferred_element_type=jn...  324 us
    unnamed x9, waiting for transfers between devices  147 us
    all_gather x1, blocking collectives, on_device(): hidden_all = lax.all_gather(hidden_own, 'seq', axis=0, tiled=True)  32.7 us
    all_gather x1, blocking collectives, on_device(): lax.all_gather(d_up_own, 'seq', axis=0, tiled=True)  26.9 us
  transfers between devices with their start and end apart: 6, of which 6 were waited for; matrix products, arithmetic and copies ran while one was open for 1% of the time, Pallas kernels for 0%

commit v1 on v0

v1 whole, which is shorter than its diff:
```python
import jax
import jax.numpy as jnp
from jax import lax
from jax.experimental import pallas as pl
from jax.experimental.pallas import tpu as pltpu
from jax.sharding import PartitionSpec as P

BF = jnp.bfloat16
F32 = jnp.float32
MESH = pl.DeviceIdType.MESH
RELATIONS = (0, 1, 2, 3)


def partner(i, relation):
    if relation == 0:
        return i
    if relation == 1:
        return lax.rem(5 - i, 4)
    if relation == 2:
        return 3 - i
    return lax.rem(i + 2, 4)


def rows16(y):
    return pl.ds(pl.multiple_of(y * 16, 16), 16)


def matmul(left, right):
    return jnp.dot(left, right, preferred_element_type=F32)


def kernel(
    t_ref, g_ref, wg_ref, wu_ref, wd_ref, mg_ref, mu_ref, md_ref,
    out_ref, gg_ref, gu_ref, gd_ref,
    xf, xt, gf, wgu, wd,
    gu_send, gu_keep, gu_core, gu_zs, gu_zk, gu_r1, gu_z2, gu_r2, gu_own,
    dh_send, dh_keep, dh_core, dh_zs, dh_zk, dh_r1, dh_z2, dh_r2,
    hf, df,
    oa_own, oa_send, oa_recv, ob_own, ob_send, ob_recv,
    a2_own, a2_send, a2_recv, b2_own, b2_send, b2_recv, o3, o3_send, o3_recv,
    send_sem, recv_sem,
):
    seq = lax.axis_index("seq")
    ffn = lax.axis_index("ffn")
    zh, core = seq // 2, lax.rem(seq, 2)
    x, zl, y = ffn // 16, lax.rem(ffn // 4, 4), lax.rem(ffn, 4)
    other = 1 - core

    def ffn_peer(rx, rz, ry):
        return (seq, partner(x, rx) * 16 + partner(zl, rz) * 4 + partner(y, ry))

    def zh_peer(relation):
        return (partner(zh, relation) * 2 + core, ffn)

    core_peer = (zh * 2 + other, ffn)

    plane = [(0, rz, ry) for rz in RELATIONS for ry in RELATIONS if (rz, ry) != (0, 0)]
    peers = [ffn_peer(*r) for r in plane] + [ffn_peer(m, 0, 0) for m in (1, 2, 3)]
    peers += [core_peer, zh_peer(1), zh_peer(2)]
    barrier = pltpu.get_barrier_semaphore()
    for peer in peers:
        pl.semaphore_signal(barrier, inc=1, device_id=peer, device_id_type=MESH)

    started = []

    def send(src, dst, peer):
        index = len(started)
        copy = pltpu.make_async_remote_copy(
            src_ref=src, dst_ref=dst, send_sem=send_sem.at[index], recv_sem=recv_sem.at[index],
            device_id=peer, device_id_type=MESH,
        )
        copy.start()
        started.append(copy)
        return copy

    for a in range(4):
        for b in range(2):
            r, c = pl.ds(a * 128, 128), pl.ds(b * 128, 128)
            wgu[r, c] = (wg_ref[r, c].astype(F32) * mg_ref[a, b].astype(F32)).astype(BF)
            wgu[r, pl.ds(256 + b * 128, 128)] = (
                wu_ref[r, c].astype(F32) * mu_ref[a, b].astype(F32)
            ).astype(BF)
            wd[c, r] = (wd_ref[c, r].astype(F32) * md_ref[b, a].astype(F32)).astype(BF)
    xf[x, zl, rows16(y), :] = t_ref[...]
    gf[x, zl, rows16(y), :] = g_ref[...]

    pl.semaphore_wait(barrier, len(peers))

    x_plane = [send(t_ref, xf.at[x, zl, rows16(y)], ffn_peer(*r)) for r in plane]
    g_z = [send(g_ref, gf.at[x, zl, rows16(y)], ffn_peer(0, r, 0)) for r in (1, 2, 3)]

    for copy in g_z:
        copy.wait_recv()
    g_block = gf.at[x, :, rows16(y)]
    g_x = [send(g_block, g_block, ffn_peer(r, 0, 0)) for r in (1, 2, 3)]
    for copy in x_plane:
        copy.wait_recv()
    x_copies = [None] + [send(xf.at[x], xf.at[x], ffn_peer(r, 0, 0)) for r in (1, 2, 3)]

    gu = dict(send=gu_send, keep=gu_keep, core=gu_core, zs=gu_zs, zk=gu_zk, r1=gu_r1, z2=gu_z2,
              r2=gu_r2, n=2, c1={}, c2={}, c3={})
    dh = dict(send=dh_send, keep=dh_keep, core=dh_core, zs=dh_zs, zk=dh_zk, r1=dh_r1, z2=dh_z2,
              r2=dh_r2, n=1, c1={}, c2={}, c3={})

    def to_core(k, j, parts):
        for t, part in enumerate(parts):
            low, high = part[:, :128], part[:, 128:]
            mine = jnp.where(core == 0, low, high).reshape(4, 64, 128)
            theirs = jnp.where(core == 0, high, low).reshape(4, 64, 128)
            k["send"][j, t] = theirs.astype(BF)
            k["keep"][j, t] = mine
        k["c1"][j] = send(k["send"].at[j], k["core"].at[j], core_peer)

    def to_z1(k, j):
        k["c1"][j].wait_recv()
        k["c2"][j] = []
        for h in (0, 1):
            r = pl.ds(32 * h, 32)
            first, second = (1, 2) if h == 0 else (2, 1)
            for t in range(k["n"]):
                for slot, (keep, relation) in enumerate(
                    ((False, first), (False, 3), (True, 0), (True, second))
                ):
                    b = partner(zh, relation)
                    value = k["keep"][j, t, b, r, :] + k["core"][j, t, b, r, :].astype(F32)
                    if keep:
                        k["zk"][j, h, t, slot - 2] = value
                    else:
                        k["zs"][j, h, t, slot] = value.astype(BF)
            k["c2"][j].append(send(k["zs"].at[j, h], k["r1"].at[j, h], zh_peer(first)))

    def to_z2(k, j):
        k["c3"][j] = []
        for h in (0, 1):
            k["c2"][j][h].wait_recv()
            for t in range(k["n"]):
                k["z2"][j, h, t] = (k["zk"][j, h, t, 1] + k["r1"][j, h, t, 1].astype(F32)).astype(BF)
            k["c3"][j].append(send(k["z2"].at[j, h], k["r2"].at[j, h], zh_peer(2 if h == 0 else 1)))

    def owned(k, j, h, t):
        return (
            k["zk"][j, h, t, 0] + k["r1"][j, h, t, 0].astype(F32) + k["r2"][j, h, t].astype(F32)
        )

    def gather1(full, j):
        mine = full.at[j, core, :, zh]
        return [send(mine, mine, zh_peer(r)) for r in (1, 2)]

    def gather2(full, j, copies):
        result = []
        for h, (relation, onward) in enumerate(((1, 2), (2, 1))):
            copies[h].wait_recv()
            block = full.at[j, core, :, partner(zh, relation), pl.ds(32 * h, 32)]
            result.append(send(block, block, zh_peer(onward)))
        return result

    def gather3(full, j, copies):
        for copy in copies:
            copy.wait_recv()
        return send(full.at[j, core], full.at[j, core], core_peer)

    def gu_compute(j):
        if j:
            x_copies[j].wait_recv()
        chunk = xf[partner(x, j)].reshape(256, 512)
        both = matmul(chunk, wgu[...])
        to_core(gu, j, [both[:, :256], both[:, 256:]])

    def transpose_x(j):
        xt[j] = xf[partner(x, j)].reshape(256, 512).T

    h1, h2, h3, d1, d2, d3 = ({} for _ in range(6))

    def gu_final(j):
        for h in (0, 1):
            gu["c3"][j][h].wait_recv()
            gate, up = owned(gu, j, h, 0), owned(gu, j, h, 1)
            sig = 1.0 / (1.0 + jnp.exp(-gate))
            hf[j, core, 0, zh, pl.ds(32 * h, 32), :] = (gate * sig * up).astype(BF)
            gu_own[j, h, 0] = gate
            gu_own[j, h, 1] = up
        h1[j] = gather1(hf, j)

    def dh_compute(j):
        chunk = gf[partner(x, j)].reshape(256, 512)
        to_core(dh, j, [lax.dot_general(chunk, wd[...], (((1,), (1,)), ((), ())), preferred_element_type=F32)])

    def dh_final(j):
        for h in (0, 1):
            dh["c3"][j][h].wait_recv()
            d_hidden, gate, up = owned(dh, j, h, 0), gu_own[j, h, 0], gu_own[j, h, 1]
            sig = 1.0 / (1.0 + jnp.exp(-gate))
            d_gate = d_hidden * up * sig * (1.0 + gate * (1.0 - sig))
            d_up = d_hidden * (gate * sig)
            df[j, core, 0, zh, pl.ds(32 * h, 32), :] = d_gate.astype(BF)
            df[j, core, 1, zh, pl.ds(32 * h, 32), :] = d_up.astype(BF)
        d1[j] = gather1(df, j)

    def h_go2(j):
        h2[j] = gather2(hf, j, h1[j])

    def h_go3(j):
        h3[j] = gather3(hf, j, h2[j])

    def d_go2(j):
        d2[j] = gather2(df, j, d1[j])

    def d_go3(j):
        d3[j] = gather3(df, j, d2[j])

    oa, ob = {}, {}

    def h_final(j):
        h3[j].wait_recv()
        hidden = jnp.concatenate(
            [hf[j, 0, 0].reshape(256, 128), hf[j, 1, 0].reshape(256, 128)], axis=1
        )
        part = matmul(hidden, wd[...])
        a, b = part[:, :256].reshape(4, 64, 256), part[:, 256:].reshape(4, 64, 256)
        if j == 0:
            oa_own[...] = a
        else:
            oa_send[j - 1] = a.astype(BF)
            oa[j] = send(oa_send.at[j - 1], oa_recv.at[j - 1], ffn_peer(j, 0, 0))
        ob_send[j] = b.astype(BF)
        ob[j] = [
            send(ob_send.at[j, :, rows16(partner(y, r))], ob_recv.at[j, r - 1], ffn_peer(0, 0, r))
            for r in (1, 2, 3)
        ]
        chunk = gf[partner(x, j)].reshape(256, 512)
        term = lax.dot_general(hidden, chunk, (((0,), (0,)), ((), ())), preferred_element_type=F32)
        if j == 0:
            gd_ref[...] = term
        else:
            gd_ref[...] += term

    a2, b2, z3 = {}, {}, {}

    def out_second():
        for j in (1, 2, 3):
            oa[j].wait_recv()
        total = oa_own[...]
        for j in range(3):
            total += oa_recv[j].astype(F32)
        oa_own[...] = total
        a2_send[...] = total.astype(BF)
        for r in (1, 2, 3):
            a2[r] = send(a2_send.at[:, rows16(partner(y, r))], a2_recv.at[r - 1], ffn_peer(0, 0, r))
        for j in range(4):
            for copy in ob[j]:
                copy.wait_recv()
            total = ob_send[j, :, rows16(y), :].astype(F32)
            for r in range(3):
                total += ob_recv[j, r].astype(F32)
            if j == 0:
                b2_own[...] = total
            else:
                b2_send[j - 1] = total.astype(BF)
                b2[j] = send(b2_send.at[j - 1], b2_recv.at[j - 1], ffn_peer(j, 0, 0))

    def out_third():
        for r in (1, 2, 3):
            a2[r].wait_recv()
            b2[r].wait_recv()
        left, right = oa_own[:, rows16(y), :], b2_own[...]
        for r in range(3):
            left += a2_recv[r].astype(F32)
            right += b2_recv[r].astype(F32)
        o3[:, :, :256] = left
        o3[:, :, 256:] = right
        o3_send[...] = o3[...].astype(BF)
        for r in (1, 2, 3):
            z3[r] = send(o3_send.at[partner(zl, r)], o3_recv.at[r - 1], ffn_peer(0, r, 0))

    def out_final():
        total = o3[zl]
        for r in (1, 2, 3):
            z3[r].wait_recv()
            total += o3_recv[r - 1].astype(F32)
        out_ref[...] = total.astype(BF)

    def d_final(j):
        d3[j].wait_recv()
        for t, ref in enumerate((gg_ref, gu_ref)):
            grad = jnp.concatenate(
                [df[j, 0, t].reshape(256, 128), df[j, 1, t].reshape(256, 128)], axis=1
            )
            term = matmul(xt[j], grad)
            if j == 0:
                ref[...] = term
            else:
                ref[...] += term

    def g_to_y():
        for copy in g_x:
            copy.wait_recv()
        column = gf.at[:, :, rows16(y)]
        return [send(column, column, ffn_peer(0, 0, r)) for r in (1, 2, 3)]

    gu_compute(0)
    g_y = g_to_y()
    to_z1(gu, 0)
    transpose_x(0)
    gu_compute(1)
    to_z1(gu, 1)
    to_z2(gu, 0)
    transpose_x(1)
    gu_compute(2)
    to_z1(gu, 2)
    to_z2(gu, 1)
    gu_final(0)
    transpose_x(2)
    gu_compute(3)
    to_z1(gu, 3)
    to_z2(gu, 2)
    gu_final(1)
    transpose_x(3)
    for copy in g_y:
        copy.wait_recv()
    dh_compute(0)
    dh_compute(1)
    to_z2(gu, 3)
    to_z1(dh, 0)
    dh_compute(2)
    dh_compute(3)
    h_go2(0)
    gu_final(2)
    to_z1(dh, 1)
    h_go2(1)
    gu_final(3)
    to_z1(dh, 2)
    to_z1(dh, 3)
    to_z2(dh, 0)
    h_go3(0)
    h_go2(2)
    to_z2(dh, 1)
    h_go3(1)
    h_go2(3)
    to_z2(dh, 2)
    to_z2(dh, 3)
    dh_final(0)
    h_final(0)
    dh_final(1)
    h_final(1)
    h_go3(2)
    h_go3(3)
    dh_final(2)
    d_go2(0)
    dh_final(3)
    d_go2(1)
    h_final(2)
    h_final(3)
    d_go3(0)
    d_go2(2)
    d_go3(1)
    d_go2(3)
    for a in range(2):
        for b in range(4):
            r, c = pl.ds(a * 128, 128), pl.ds(b * 128, 128)
            gd_ref[r, c] = gd_ref[r, c] * md_ref[a, b].astype(F32)
    out_second()
    d_final(0)
    d_go3(2)
    d_final(1)
    d_go3(3)
    out_third()
    d_final(2)
    d_final(3)
    for a in range(4):
        for b in range(2):
            r, c = pl.ds(a * 128, 128), pl.ds(b * 128, 128)
            gg_ref[r, c] = gg_ref[r, c] * mg_ref[a, b].astype(F32)
            gu_ref[r, c] = gu_ref[r, c] * mu_ref[a, b].astype(F32)
    out_final()
    for copy in started:
        copy.wait_send()


def reduce_scratch(n):
    return [
        pltpu.VMEM((4, n, 4, 64, 128), BF),
        pltpu.VMEM((4, n, 4, 64, 128), F32),
        pltpu.VMEM((4, n, 4, 64, 128), BF),
        pltpu.VMEM((4, 2, n, 2, 32, 128), BF),
        pltpu.VMEM((4, 2, n, 2, 32, 128), F32),
        pltpu.VMEM((4, 2, n, 2, 32, 128), BF),
        pltpu.VMEM((4, 2, n, 32, 128), BF),
        pltpu.VMEM((4, 2, n, 32, 128), BF),
    ]


COPIES = 160


def on_device(*args):
    vmem = pl.BlockSpec(memory_space=pltpu.VMEM)
    smem = pl.BlockSpec(memory_space=pltpu.SMEM)
    return pl.pallas_call(
        kernel,
        out_shape=(
            jax.ShapeDtypeStruct((16, 512), BF),
            jax.ShapeDtypeStruct((512, 256), F32),
            jax.ShapeDtypeStruct((512, 256), F32),
            jax.ShapeDtypeStruct((256, 512), F32),
        ),
        in_specs=[vmem] * 5 + [smem] * 3,
        out_specs=(vmem,) * 4,
        scratch_shapes=[
            pltpu.VMEM((4, 4, 64, 512), BF),
            pltpu.VMEM((4, 512, 256), BF),
            pltpu.VMEM((4, 4, 64, 512), BF),
            pltpu.VMEM((512, 512), BF),
            pltpu.VMEM((256, 512), BF),
            *reduce_scratch(2),
            pltpu.VMEM((4, 2, 2, 32, 128), F32),
            *reduce_scratch(1),
            pltpu.VMEM((4, 2, 1, 4, 64, 128), BF),
            pltpu.VMEM((4, 2, 2, 4, 64, 128), BF),
            pltpu.VMEM((4, 64, 256), F32),
            pltpu.VMEM((3, 4, 64, 256), BF),
            pltpu.VMEM((3, 4, 64, 256), BF),
            pltpu.VMEM((4, 16, 256), F32),
            pltpu.VMEM((4, 4, 64, 256), BF),
            pltpu.VMEM((4, 3, 4, 16, 256), BF),
            pltpu.VMEM((4, 16, 256), F32),
            pltpu.VMEM((4, 64, 256), BF),
            pltpu.VMEM((3, 4, 16, 256), BF),
            pltpu.VMEM((4, 16, 256), F32),
            pltpu.VMEM((3, 4, 16, 256), BF),
            pltpu.VMEM((3, 4, 16, 256), BF),
            pltpu.VMEM((4, 16, 512), F32),
            pltpu.VMEM((4, 16, 512), BF),
            pltpu.VMEM((3, 16, 512), BF),
            pltpu.SemaphoreType.DMA((COPIES,)),
            pltpu.SemaphoreType.DMA((COPIES,)),
        ],
        compiler_params=pltpu.CompilerParams(
            collective_id=0, has_side_effects=True, vmem_limit_bytes=48 * 2**20
        ),
        cost_estimate=pl.CostEstimate(flops=1_700_000_000, bytes_accessed=2_500_000, transcendentals=100_000),
    )(*args)


def solution(mesh):
    return jax.shard_map(
        on_device,
        mesh=mesh,
        in_specs=(
            P("ffn", "seq"),
            P("ffn", "seq"),
            P("seq", "ffn"),
            P("seq", "ffn"),
            P("ffn", "seq"),
            P("seq", "ffn"),
            P("seq", "ffn"),
            P("ffn", "seq"),
        ),
        out_specs=(P("ffn", "seq"), P("seq", "ffn"), P("seq", "ffn"), P("ffn", "seq")),
        check_vma=False,
    )
```

time: 1290 us -> 114 us (0.09)
  the two profiles are of different devices: /device:TPU:128 before, /device:TPU:1 now
where the time goes in v1:
time: 114 us; the launch traced here: 113 us
  Pallas kernels  103 us (90%)
  local copies, waits for them, and re-layouts  8.72 us (8%)
    pallas_call x1, Pallas kernels, on_device(): pl.pallas_call(kernel, out_shape=(jax.ShapeDtypeStruct((16, 512), BF), ja...  103 us
    unnamed x20, local copies, waits for them, and re-layouts  8.72 us

profile of v1, /device:TPU:1, one launch (start us, length us, event | category | flops | bytes accessed | tf_op | source)
XLA Modules:
  0.0 112.6 jit_solution(7005679610732957671)
XLA Ops:
  0.6 0.0 copy-start.6
  0.6 0.8 copy.12.mg_ref
  1.4 0.0 copy-done.6
  1.4 0.0 copy-start.5
  1.4 0.1 copy.13.mu_ref
  1.5 0.6 copy-done.5
  2.1 0.0 copy-start
  2.1 0.9 copy-done
  3.0 0.0 copy-start.1
  3.0 0.9 copy-done.1
  4.0 0.0 copy-start.2
  4.0 0.9 copy-done.2
  4.9 0.0 copy-start.3
  4.9 0.7 copy-done.3
  5.7 0.0 copy-start.4
  5.7 0.7 copy-done.4
  6.4 103.3 %shard_map.111 = (bf16[16,512]{1,0:T(8,128)(2,1)S(1)}, f32[512,256]{1,0:T(8,128)S(1)}, f32[512,256]{1,0:T(8,128)S(1)}, f32[256,512]{1,0:T(8,128)S(1)}) custom-call(bf16[16,512]{1,0:T(8,128)(2,1)S(1)} %copy-done.3, bf16[16,512]{1,0:T(8,128)(2,1)S(1)} %copy-done.4, bf16[512,256]{1,0:T(8,128)(2,1)S(1)} %copy-done, bf16[512,256]{1,0:T(8,128)(2,1)S(1)} %copy-done.1, ...), custom_call_target="tpu_custom_call" | custom-call | flops 1700000000 | bytes 2500000 | tf_op jit(solution)/shard_map/pallas_call | solution.py:398
  109.7 0.6 copy.18
  110.3 0.8 copy.19
  111.1 0.8 copy.20
  111.8 0.8 copy.21
Async XLA Ops:
  0.6 0.8 copy-start.6
  1.4 0.7 copy-start.5
  2.1 0.9 copy-start
  3.0 0.9 copy-start.1
  4.0 0.9 copy-start.2
  4.9 0.7 copy-start.3
  5.7 0.7 copy-start.4

commit v2 on v1

--- a/solution.py
+++ b/solution.py
@@ -30,15 +30,15 @@
 
 
 def kernel(
-    t_ref, g_ref, wg_ref, wu_ref, wd_ref, mg_ref, mu_ref, md_ref,
+    t_ref, g_ref, wg_ref, wu_ref, wd_ref, mgt_ref, mut_ref, mdt_ref,
     out_ref, gg_ref, gu_ref, gd_ref,
-    xf, xt, gf, wgu, wd,
+    wg_raw, wu_raw, wd_raw, mg, mu, md, xf, xt, gf, wgu, wd, wdp,
     gu_send, gu_keep, gu_core, gu_zs, gu_zk, gu_r1, gu_z2, gu_r2, gu_own,
     dh_send, dh_keep, dh_core, dh_zs, dh_zk, dh_r1, dh_z2, dh_r2,
     hf, df,
     oa_own, oa_send, oa_recv, ob_own, ob_send, ob_recv,
     a2_own, a2_send, a2_recv, b2_own, b2_send, b2_recv, o3, o3_send, o3_recv,
-    send_sem, recv_sem,
+    send_sem, recv_sem, load_sem,
 ):
     seq = lax.axis_index("seq")
     ffn = lax.axis_index("ffn")
@@ -54,8 +54,7 @@
 
     core_peer = (zh * 2 + other, ffn)
 
-    plane = [(0, rz, ry) for rz in RELATIONS for ry in RELATIONS if (rz, ry) != (0, 0)]
-    peers = [ffn_peer(*r) for r in plane] + [ffn_peer(m, 0, 0) for m in (1, 2, 3)]
+    peers = [ffn_peer(*r) for m in (1, 2, 3) for r in ((m, 0, 0), (0, m, 0), (0, 0, m))]
     peers += [core_peer, zh_peer(1), zh_peer(2)]
     barrier = pltpu.get_barrier_semaphore()
     for peer in peers:
@@ -73,42 +72,67 @@
         started.append(copy)
         return copy
 
-    for a in range(4):
-        for b in range(2):
+    x_own, g_own = xf.at[x, zl, rows16(y)], gf.at[x, zl, rows16(y)]
+    loads = [
+        pltpu.make_async_copy(src, dst, load_sem.at[i])
+        for i, (src, dst) in enumerate((
+            (t_ref, x_own), (g_ref, g_own), (mgt_ref, mg), (mut_ref, mu), (mdt_ref, md),
+            (wg_ref, wg_raw), (wu_ref, wu_raw), (wd_ref, wd_raw),
+        ))
+    ]
+    for load in loads:
+        load.start()
+    for load in loads:
+        load.wait()
+
+    for b in range(2):
+        place = lax.rem(b + core, 2)
+        for a in range(4):
             r, c = pl.ds(a * 128, 128), pl.ds(b * 128, 128)
-            wgu[r, c] = (wg_ref[r, c].astype(F32) * mg_ref[a, b].astype(F32)).astype(BF)
-            wgu[r, pl.ds(256 + b * 128, 128)] = (
-                wu_ref[r, c].astype(F32) * mu_ref[a, b].astype(F32)
-            ).astype(BF)
-            wd[c, r] = (wd_ref[c, r].astype(F32) * md_ref[b, a].astype(F32)).astype(BF)
-    xf[x, zl, rows16(y), :] = t_ref[...]
-    gf[x, zl, rows16(y), :] = g_ref[...]
+            for t, (raw, mask) in enumerate(((wg_raw, mg), (wu_raw, mu))):
+                kept = (raw[r, c].astype(F32) * mask[b, a].astype(F32)).astype(BF)
+                wgu[r, pl.ds(pl.multiple_of(place * 256 + t * 128, 128), 128)] = kept
+            kept = (wd_raw[c, r].astype(F32) * md[b, a].astype(F32)).astype(BF)
+            wd[c, r] = kept
+            wdp[pl.ds(pl.multiple_of(place * 128, 128), 128), r] = kept
 
     pl.semaphore_wait(barrier, len(peers))
 
-    x_plane = [send(t_ref, xf.at[x, zl, rows16(y)], ffn_peer(*r)) for r in plane]
-    g_z = [send(g_ref, gf.at[x, zl, rows16(y)], ffn_peer(0, r, 0)) for r in (1, 2, 3)]
-
-    for copy in g_z:
-        copy.wait_recv()
-    g_block = gf.at[x, :, rows16(y)]
-    g_x = [send(g_block, g_block, ffn_peer(r, 0, 0)) for r in (1, 2, 3)]
-    for copy in x_plane:
-        copy.wait_recv()
-    x_copies = [None] + [send(xf.at[x], xf.at[x], ffn_peer(r, 0, 0)) for r in (1, 2, 3)]
+    def landed(*copies):
+        for copy in copies:
+            if not any(copy is old for old in arrived):
+                arrived.append(copy)
+                copy.wait_recv()
+
+    arrived = []
+    x_z = [send(x_own, x_own, ffn_peer(0, r, 0)) for r in (1, 2, 3)]
+    g_z = [send(g_own, g_own, ffn_peer(0, r, 0)) for r in (1, 2, 3)]
+    x_flow, g_flow = {}, {}
+    left, right = pl.ds(0, 256), pl.ds(256, 256)
+
+    def spread(column, rows, flow):
+        landed(*column)
+        a, b = rows.at[x, :, rows16(y), left], rows.at[x, :, rows16(y), right]
+        flow["a"] = [send(a, a, ffn_peer(0, 0, r)) for r in (1, 2, 3)]
+        flow["b"] = [send(b, b, ffn_peer(r, 0, 0)) for r in (1, 2, 3)]
+
+    def complete(rows, flow):
+        landed(*flow["a"])
+        a, b = rows.at[x, :, :, left], rows.at[:, :, rows16(y), right]
+        flow["all"] = [send(a, a, ffn_peer(r, 0, 0)) for r in (1, 2, 3)]
+        landed(*flow["b"])
+        flow["all"] += [send(b, b, ffn_peer(0, 0, r)) for r in (1, 2, 3)]
 
     gu = dict(send=gu_send, keep=gu_keep, core=gu_core, zs=gu_zs, zk=gu_zk, r1=gu_r1, z2=gu_z2,
               r2=gu_r2, n=2, c1={}, c2={}, c3={})
     dh = dict(send=dh_send, keep=dh_keep, core=dh_core, zs=dh_zs, zk=dh_zk, r1=dh_r1, z2=dh_z2,
               r2=dh_r2, n=1, c1={}, c2={}, c3={})
 
-    def to_core(k, j, parts):
-        for t, part in enumerate(parts):
-            low, high = part[:, :128], part[:, 128:]
-            mine = jnp.where(core == 0, low, high).reshape(4, 64, 128)
-            theirs = jnp.where(core == 0, high, low).reshape(4, 64, 128)
-            k["send"][j, t] = theirs.astype(BF)
-            k["keep"][j, t] = mine
+    def to_core(k, j, both):
+        n = k["n"]
+        for t in range(n):
+            k["send"][j, t] = both[:, 128 * (n + t):128 * (n + t + 1)].reshape(4, 64, 128).astype(BF)
+            k["keep"][j, t] = both[:, 128 * t:128 * (t + 1)].reshape(4, 64, 128)
         k["c1"][j] = send(k["send"].at[j], k["core"].at[j], core_peer)
 
     def to_z1(k, j):
@@ -160,11 +184,8 @@
         return send(full.at[j, core], full.at[j, core], core_peer)
 
     def gu_compute(j):
-        if j:
-            x_copies[j].wait_recv()
-        chunk = xf[partner(x, j)].reshape(256, 512)
-        both = matmul(chunk, wgu[...])
-        to_core(gu, j, [both[:, :256], both[:, 256:]])
+        landed(*x_flow["all"])
+        to_core(gu, j, matmul(xf[partner(x, j)].reshape(256, 512), wgu[...]))
 
     def transpose_x(j):
         xt[j] = xf[partner(x, j)].reshape(256, 512).T
@@ -182,8 +203,11 @@
         h1[j] = gather1(hf, j)
 
     def dh_compute(j):
+        landed(*g_flow["all"])
         chunk = gf[partner(x, j)].reshape(256, 512)
-        to_core(dh, j, [lax.dot_general(chunk, wd[...], (((1,), (1,)), ((), ())), preferred_element_type=F32)])
+        to_core(dh, j, lax.dot_general(
+            chunk, wdp[...], (((1,), (1,)), ((), ())), preferred_element_type=F32
+        ))
 
     def dh_final(j):
         for h in (0, 1):
@@ -209,6 +233,8 @@
         d3[j] = gather3(df, j, d2[j])
 
     oa, ob = {}, {}
+    h_done, d_done = [], []
+    h_done, d_done = [], []
 
     def h_final(j):
         h3[j].wait_recv()
@@ -229,10 +255,16 @@
         ]
         chunk = gf[partner(x, j)].reshape(256, 512)
         term = lax.dot_general(hidden, chunk, (((0,), (0,)), ((), ())), preferred_element_type=F32)
-        if j == 0:
+        if h_done:
+            term += gd_ref[...]
+        h_done.append(j)
+        if len(h_done) < 4:
             gd_ref[...] = term
-        else:
-            gd_ref[...] += term
+            return
+        for a in range(2):
+            for b in range(4):
+                r, c = slice(a * 128, a * 128 + 128), slice(b * 128, b * 128 + 128)
+                gd_ref[r, c] = term[r, c] * md[a, b].astype(F32)
 
     a2, b2, z3 = {}, {}, {}
 
@@ -281,99 +313,105 @@
 
     def d_final(j):
         d3[j].wait_recv()
-        for t, ref in enumerate((gg_ref, gu_ref)):
+        for t, (ref, mask) in enumerate(((gg_ref, mg), (gu_ref, mu))):
             grad = jnp.concatenate(
                 [df[j, 0, t].reshape(256, 128), df[j, 1, t].reshape(256, 128)], axis=1
             )
             term = matmul(xt[j], grad)
-            if j == 0:
+            if d_done:
+                term += ref[...]
+            if len(d_done) < 3:
                 ref[...] = term
-            else:
-                ref[...] += term
-
-    def g_to_y():
-        for copy in g_x:
-            copy.wait_recv()
-        column = gf.at[:, :, rows16(y)]
-        return [send(column, column, ffn_peer(0, 0, r)) for r in (1, 2, 3)]
-
+                continue
+            for a in range(4):
+                for b in range(2):
+                    r, c = slice(a * 128, a * 128 + 128), slice(b * 128, b * 128 + 128)
+                    ref[r, c] = term[r, c] * mask[b, a].astype(F32)
+        d_done.append(j)
+        d_done.append(j)
+
+    spread(x_z, xf, x_flow)
+    complete(xf, x_flow)
     gu_compute(0)
-    g_y = g_to_y()
+    gu_compute(1)
+    gu_compute(2)
+    gu_compute(3)
+    spread(g_z, gf, g_flow)
     to_z1(gu, 0)
+    to_z1(gu, 1)
+    to_z1(gu, 2)
+    to_z1(gu, 3)
+    complete(gf, g_flow)
     transpose_x(0)
-    gu_compute(1)
-    to_z1(gu, 1)
+    transpose_x(1)
+    transpose_x(2)
+    transpose_x(3)
     to_z2(gu, 0)
-    transpose_x(1)
-    gu_compute(2)
-    to_z1(gu, 2)
     to_z2(gu, 1)
-    gu_final(0)
-    transpose_x(2)
-    gu_compute(3)
-    to_z1(gu, 3)
     to_z2(gu, 2)
-    gu_final(1)
-    transpose_x(3)
-    for copy in g_y:
-        copy.wait_recv()
+    to_z2(gu, 3)
     dh_compute(0)
     dh_compute(1)
-    to_z2(gu, 3)
-    to_z1(dh, 0)
     dh_compute(2)
     dh_compute(3)
+    gu_final(0)
+    gu_final(1)
+    to_z1(dh, 0)
+    to_z1(dh, 1)
+    gu_final(2)
+    to_z1(dh, 2)
+    gu_final(3)
+    to_z1(dh, 3)
     h_go2(0)
-    gu_final(2)
-    to_z1(dh, 1)
     h_go2(1)
-    gu_final(3)
-    to_z1(dh, 2)
-    to_z1(dh, 3)
+    h_go2(2)
+    h_go2(3)
     to_z2(dh, 0)
     h_go3(0)
-    h_go2(2)
     to_z2(dh, 1)
     h_go3(1)
-    h_go2(3)
     to_z2(dh, 2)
     to_z2(dh, 3)
-    dh_final(0)
     h_final(0)
-    dh_final(1)
     h_final(1)
     h_go3(2)
     h_go3(3)
-    dh_final(2)
-    d_go2(0)
-    dh_final(3)
-    d_go2(1)
     h_final(2)
     h_final(3)
+    dh_final(0)
+    dh_final(1)
+    dh_final(2)
+    dh_final(3)
+    out_second()
+    d_go2(0)
+    d_go2(1)
+    d_go2(2)
+    d_go2(3)
+    out_third()
     d_go3(0)
-    d_go2(2)
     d_go3(1)
-    d_go2(3)
-    for a in range(2):
-        for b in range(4):
-            r, c = pl.ds(a * 128, 128), pl.ds(b * 128, 128)
-            gd_ref[r, c] = gd_ref[r, c] * md_ref[a, b].astype(F32)
-    out_second()
     d_final(0)
     d_go3(2)
     d_final(1)
     d_go3(3)
-    out_third()
+    out_final()
     d_final(2)
     d_final(3)
-    for a in range(4):
-        for b in range(2):
-            r, c = pl.ds(a * 128, 128), pl.ds(b * 128, 128)
-            gg_ref[r, c] = gg_ref[r, c] * mg_ref[a, b].astype(F32)
-            gu_ref[r, c] = gu_ref[r, c] * mu_ref[a, b].astype(F32)
-    out_final()
     for copy in started:
         copy.wait_send()
+
+
+def hand_over(*refs):
+    source, result, held, sem = refs[:4], refs[4:8], refs[8:12], refs[12]
+    loads = [pltpu.make_async_copy(source[i], held[i], sem.at[0, i]) for i in range(4)]
+    stores = [pltpu.make_async_copy(held[i], result[i], sem.at[1, i]) for i in range(4)]
+    for load in loads:
+        load.start()
+    for load, store in zip(loads, stores):
+        load.wait()
+        store.start()
+    for store in stores:
+        store.wait()
 
 
 def reduce_scratch(n):
@@ -392,10 +430,11 @@
 COPIES = 160
 
 
-def on_device(*args):
+def on_device(teacher_rows, grad_out, w_gate, w_up, w_down, mask_gate, mask_up, mask_down):
+    args = (teacher_rows, grad_out, w_gate, w_up, w_down, mask_gate.T, mask_up.T, mask_down)
     vmem = pl.BlockSpec(memory_space=pltpu.VMEM)
-    smem = pl.BlockSpec(memory_space=pltpu.SMEM)
-    return pl.pallas_call(
+    hbm = pl.BlockSpec(memory_space=pltpu.HBM)
+    results = pl.pallas_call(
         kernel,
         out_shape=(
             jax.ShapeDtypeStruct((16, 512), BF),
@@ -403,13 +442,18 @@
             jax.ShapeDtypeStruct((512, 256), F32),
             jax.ShapeDtypeStruct((256, 512), F32),
         ),
-        in_specs=[vmem] * 5 + [smem] * 3,
+        in_specs=[hbm] * 8,
         out_specs=(vmem,) * 4,
         scratch_shapes=[
+            pltpu.VMEM((512, 256), BF),
+            pltpu.VMEM((512, 256), BF),
+            pltpu.VMEM((256, 512), BF),
+            *[pltpu.SMEM((2, 4), jnp.int32)] * 3,
             pltpu.VMEM((4, 4, 64, 512), BF),
             pltpu.VMEM((4, 512, 256), BF),
             pltpu.VMEM((4, 4, 64, 512), BF),
             pltpu.VMEM((512, 512), BF),
+            pltpu.VMEM((256, 512), BF),
             pltpu.VMEM((256, 512), BF),
             *reduce_scratch(2),
             pltpu.VMEM((4, 2, 2, 32, 128), F32),
@@ -433,12 +477,21 @@
             pltpu.VMEM((3, 16, 512), BF),
             pltpu.SemaphoreType.DMA((COPIES,)),
             pltpu.SemaphoreType.DMA((COPIES,)),
+            pltpu.SemaphoreType.DMA((8,)),
         ],
         compiler_params=pltpu.CompilerParams(
-            collective_id=0, has_side_effects=True, vmem_limit_bytes=48 * 2**20
+            collective_id=0, has_side_effects=True, vmem_limit_bytes=62 * 2**20
         ),
         cost_estimate=pl.CostEstimate(flops=1_700_000_000, bytes_accessed=2_500_000, transcendentals=100_000),
     )(*args)
+    return pl.pallas_call(
+        hand_over,
+        out_shape=tuple(jax.ShapeDtypeStruct(r.shape, r.dtype) for r in results),
+        in_specs=[hbm] * 4,
+        out_specs=(hbm,) * 4,
+        scratch_shapes=[*[pltpu.VMEM(r.shape, r.dtype) for r in results], pltpu.SemaphoreType.DMA((2, 4))],
+        compiler_params=pltpu.CompilerParams(vmem_limit_bytes=62 * 2**20),
+    )(*results)
 
 
 def solution(mesh):

time: 114 us -> 103 us (0.904); the launches traced: 113 us -> 103 us
  local copies, waits for them, and re-layouts: 8.72 us -> 0 us
    unnamed x20 -> x0, local copies, waits for them, and re-layouts: 8.72 us -> none
    pallas_call x1, Pallas kernels: 103 us -> 100 us  [on_device(): pl.pallas_call(kernel, out_shape=(jax.ShapeDtypeStruct((16, 512), BF), ja...]
    pallas_call x0 -> x1, Pallas kernels: none -> 2.27 us  [on_device(): pl.pallas_call(hand_over, out_shape=tuple((jax.ShapeDtypeStruct(r.shape,...]
where the time goes in v2:
time: 103 us
  Pallas kernels  103 us (100%)
    pallas_call x1, Pallas kernels, on_device(): pl.pallas_call(kernel, out_shape=(jax.ShapeDtypeStruct((16, 512), BF), ja...  100 us
    pallas_call x1, Pallas kernels, on_device(): pl.pallas_call(hand_over, out_shape=tuple((jax.ShapeDtypeStruct(r.shape,...  2.27 us

profile of v2, /device:TPU:1, one launch (start us, length us, event | category | flops | bytes accessed | tf_op | source)
XLA Modules:
  0.0 103.1 jit_solution(1194746495842549259)
XLA Ops:
  0.6 100.2 %shard_map.111 = (bf16[16,512]{1,0:T(8,128)(2,1)}, f32[512,256]{1,0:T(8,128)}, f32[512,256]{1,0:T(8,128)}, f32[256,512]{1,0:T(8,128)}) custom-call(bf16[16,512]{1,0:T(8,128)(2,1)} %t_ref.1, bf16[16,512]{1,0:T(8,128)(2,1)} %g_ref.1, bf16[512,256]{1,0:T(8,128)(2,1)} %wg_ref.1, bf16[512,256]{1,0:T(8,128)(2,1)} %wu_ref.1, bf16[256,512]{1,0:T(8,128)(2,1)} %wd_ref.1, ...), custom_call_target="tpu_custom_call" | custom-call | flops 1700000000 | bytes 2500000 | tf_op jit(solution)/shard_map/pallas_call | solution.py:437
  100.9 2.3 %shard_map.112 = (bf16[16,512]{1,0:T(8,128)(2,1)}, f32[512,256]{1,0:T(8,128)}, f32[512,256]{1,0:T(8,128)}, f32[256,512]{1,0:T(8,128)}) custom-call(bf16[16,512]{1,0:T(8,128)(2,1)} %get-tuple-element.8.refs_0_, f32[512,256]{1,0:T(8,128)} %get-tuple-element.9.refs_1_, f32[512,256]{1,0:T(8,128)} %get-tuple-element.10.refs_2_, f32[256,512]{1,0:T(8,128)} %get-tuple-element.11.refs_3_), custom_call_target="tpu_custom_call" | custom-call | tf_op jit(solution)/shard_map/pallas_call | solution.py:487

commit v3 on v2

--- a/solution.py
+++ b/solution.py
@@ -112,16 +112,19 @@
 
     def spread(column, rows, flow):
         landed(*column)
-        a, b = rows.at[x, :, rows16(y), left], rows.at[x, :, rows16(y), right]
-        flow["a"] = [send(a, a, ffn_peer(0, 0, r)) for r in (1, 2, 3)]
+        a, b = rows.at[x, :, rows16(y)], rows.at[x, :, rows16(y), right]
+        flow[0] = [send(a, a, ffn_peer(0, 0, r)) for r in (1, 2, 3)]
         flow["b"] = [send(b, b, ffn_peer(r, 0, 0)) for r in (1, 2, 3)]
 
     def complete(rows, flow):
-        landed(*flow["a"])
-        a, b = rows.at[x, :, :, left], rows.at[:, :, rows16(y), right]
-        flow["all"] = [send(a, a, ffn_peer(r, 0, 0)) for r in (1, 2, 3)]
-        landed(*flow["b"])
-        flow["all"] += [send(b, b, ffn_peer(0, 0, r)) for r in (1, 2, 3)]
+        for j in (1, 2, 3):
+            landed(flow["b"][j - 1])
+            b = rows.at[partner(x, j), :, rows16(y), right]
+            flow[j] = [send(b, b, ffn_peer(0, 0, r)) for r in (1, 2, 3)]
+        landed(*flow[0])
+        a = rows.at[x, :, :, left]
+        for j in (1, 2, 3):
+            flow[j].append(send(a, a, ffn_peer(j, 0, 0)))
 
     gu = dict(send=gu_send, keep=gu_keep, core=gu_core, zs=gu_zs, zk=gu_zk, r1=gu_r1, z2=gu_z2,
               r2=gu_r2, n=2, c1={}, c2={}, c3={})
@@ -184,7 +187,7 @@
         return send(full.at[j, core], full.at[j, core], core_peer)
 
     def gu_compute(j):
-        landed(*x_flow["all"])
+        landed(*x_flow[j])
         to_core(gu, j, matmul(xf[partner(x, j)].reshape(256, 512), wgu[...]))
 
     def transpose_x(j):
@@ -203,7 +206,7 @@
         h1[j] = gather1(hf, j)
 
     def dh_compute(j):
-        landed(*g_flow["all"])
+        landed(*g_flow[j])
         chunk = gf[partner(x, j)].reshape(256, 512)
         to_core(dh, j, lax.dot_general(
             chunk, wdp[...], (((1,), (1,)), ((), ())), preferred_element_type=F32
@@ -333,58 +336,58 @@
     spread(x_z, xf, x_flow)
     complete(xf, x_flow)
     gu_compute(0)
+    to_z1(gu, 0)
     gu_compute(1)
     gu_compute(2)
     gu_compute(3)
     spread(g_z, gf, g_flow)
-    to_z1(gu, 0)
     to_z1(gu, 1)
     to_z1(gu, 2)
     to_z1(gu, 3)
     complete(gf, g_flow)
+    to_z2(gu, 0)
     transpose_x(0)
     transpose_x(1)
+    to_z2(gu, 1)
     transpose_x(2)
     transpose_x(3)
-    to_z2(gu, 0)
-    to_z2(gu, 1)
     to_z2(gu, 2)
-    to_z2(gu, 3)
     dh_compute(0)
     dh_compute(1)
     dh_compute(2)
     dh_compute(3)
+    to_z2(gu, 3)
+    to_z1(dh, 0)
+    to_z1(dh, 1)
+    to_z1(dh, 2)
+    to_z1(dh, 3)
     gu_final(0)
     gu_final(1)
-    to_z1(dh, 0)
-    to_z1(dh, 1)
     gu_final(2)
-    to_z1(dh, 2)
     gu_final(3)
-    to_z1(dh, 3)
+    to_z2(dh, 0)
+    to_z2(dh, 1)
+    to_z2(dh, 2)
+    to_z2(dh, 3)
     h_go2(0)
     h_go2(1)
     h_go2(2)
     h_go2(3)
-    to_z2(dh, 0)
-    h_go3(0)
-    to_z2(dh, 1)
-    h_go3(1)
-    to_z2(dh, 2)
-    to_z2(dh, 3)
-    h_final(0)
-    h_final(1)
-    h_go3(2)
-    h_go3(3)
-    h_final(2)
-    h_final(3)
     dh_final(0)
     dh_final(1)
     dh_final(2)
     dh_final(3)
-    out_second()
+    h_go3(0)
+    h_go3(1)
+    h_go3(2)
+    h_final(0)
+    h_go3(3)
+    h_final(1)
+    h_final(2)
+    h_final(3)
     d_go2(0)
     d_go2(1)
+    out_second()
     d_go2(2)
     d_go2(3)
     out_third()

time: 103 us -> 98.9 us (0.960)
  Pallas kernels: 103 us -> 97.9 us
    pallas_call x1, Pallas kernels: 100 us -> 95.6 us  [on_device(): pl.pallas_call(kernel, out_shape=(jax.ShapeDtypeStruct((16, 512), BF), ja...]
where the time goes in v3:
time: 98.9 us; the launch traced here: 98.5 us
  Pallas kernels  97.9 us (99%)
    pallas_call x1, Pallas kernels, on_device(): pl.pallas_call(kernel, out_shape=(jax.ShapeDtypeStruct((16, 512), BF), ja...  95.6 us
    pallas_call x1, Pallas kernels, on_device(): pl.pallas_call(hand_over, out_shape=tuple((jax.ShapeDtypeStruct(r.shape,...  2.27 us

profile of v3, /device:TPU:1, one launch (start us, length us, event | category | flops | bytes accessed | tf_op | source)
XLA Modules:
  0.0 98.5 jit_solution(862560336805591020)
XLA Ops:
  0.6 95.6 %shard_map.111 = (bf16[16,512]{1,0:T(8,128)(2,1)}, f32[512,256]{1,0:T(8,128)}, f32[512,256]{1,0:T(8,128)}, f32[256,512]{1,0:T(8,128)}) custom-call(bf16[16,512]{1,0:T(8,128)(2,1)} %t_ref.1, bf16[16,512]{1,0:T(8,128)(2,1)} %g_ref.1, bf16[512,256]{1,0:T(8,128)(2,1)} %wg_ref.1, bf16[512,256]{1,0:T(8,128)(2,1)} %wu_ref.1, bf16[256,512]{1,0:T(8,128)(2,1)} %wd_ref.1, ...), custom_call_target="tpu_custom_call" | custom-call | flops 1700000000 | bytes 2500000 | tf_op jit(solution)/shard_map/pallas_call | solution.py:440
  96.3 2.3 %shard_map.112 = (bf16[16,512]{1,0:T(8,128)(2,1)}, f32[512,256]{1,0:T(8,128)}, f32[512,256]{1,0:T(8,128)}, f32[256,512]{1,0:T(8,128)}) custom-call(bf16[16,512]{1,0:T(8,128)(2,1)} %get-tuple-element.8.refs_0_, f32[512,256]{1,0:T(8,128)} %get-tuple-element.9.refs_1_, f32[512,256]{1,0:T(8,128)} %get-tuple-element.10.refs_2_, f32[256,512]{1,0:T(8,128)} %get-tuple-element.11.refs_3_), custom_call_target="tpu_custom_call" | custom-call | tf_op jit(solution)/shard_map/pallas_call | solution.py:490

commit v4 on v3

--- a/solution.py
+++ b/solution.py
@@ -82,7 +82,22 @@
     ]
     for load in loads:
         load.start()
-    for load in loads:
+    for load in loads[:2]:
+        load.wait()
+
+    pl.semaphore_wait(barrier, len(peers))
+
+    def landed(*copies):
+        for copy in copies:
+            if not any(copy is old for old in arrived):
+                arrived.append(copy)
+                copy.wait_recv()
+
+    arrived = []
+    x_z = [send(x_own, x_own, ffn_peer(0, r, 0)) for r in (1, 2, 3)]
+    g_z = [send(g_own, g_own, ffn_peer(0, r, 0)) for r in (1, 2, 3)]
+
+    for load in loads[2:]:
         load.wait()
 
     for b in range(2):
@@ -96,17 +111,6 @@
             wd[c, r] = kept
             wdp[pl.ds(pl.multiple_of(place * 128, 128), 128), r] = kept
 
-    pl.semaphore_wait(barrier, len(peers))
-
-    def landed(*copies):
-        for copy in copies:
-            if not any(copy is old for old in arrived):
-                arrived.append(copy)
-                copy.wait_recv()
-
-    arrived = []
-    x_z = [send(x_own, x_own, ffn_peer(0, r, 0)) for r in (1, 2, 3)]
-    g_z = [send(g_own, g_own, ffn_peer(0, r, 0)) for r in (1, 2, 3)]
     x_flow, g_flow = {}, {}
     left, right = pl.ds(0, 256), pl.ds(256, 256)
 
@@ -116,14 +120,14 @@
         flow[0] = [send(a, a, ffn_peer(0, 0, r)) for r in (1, 2, 3)]
         flow["b"] = [send(b, b, ffn_peer(r, 0, 0)) for r in (1, 2, 3)]
 
-    def complete(rows, flow):
-        for j in (1, 2, 3):
+    def complete(rows, flow, chunks):
+        for j in chunks:
             landed(flow["b"][j - 1])
             b = rows.at[partner(x, j), :, rows16(y), right]
             flow[j] = [send(b, b, ffn_peer(0, 0, r)) for r in (1, 2, 3)]
         landed(*flow[0])
         a = rows.at[x, :, :, left]
-        for j in (1, 2, 3):
+        for j in chunks:
             flow[j].append(send(a, a, ffn_peer(j, 0, 0)))
 
     gu = dict(send=gu_send, keep=gu_keep, core=gu_core, zs=gu_zs, zk=gu_zk, r1=gu_r1, z2=gu_z2,
@@ -334,17 +338,18 @@
         d_done.append(j)
 
     spread(x_z, xf, x_flow)
-    complete(xf, x_flow)
+    complete(xf, x_flow, (1, 2))
     gu_compute(0)
     to_z1(gu, 0)
     gu_compute(1)
+    complete(xf, x_flow, (3,))
     gu_compute(2)
+    to_z1(gu, 1)
+    to_z1(gu, 2)
     gu_compute(3)
     spread(g_z, gf, g_flow)
-    to_z1(gu, 1)
-    to_z1(gu, 2)
     to_z1(gu, 3)
-    complete(gf, g_flow)
+    complete(gf, g_flow, (1, 2, 3))
     to_z2(gu, 0)
     transpose_x(0)
     transpose_x(1)

time: 98.9 us -> 98.5 us (level)
  no operation moved by 1% of the time
where the time goes in v4:
time: 98.5 us; the launch traced here: 98.1 us
  Pallas kernels  97.4 us (99%)
    pallas_call x1, Pallas kernels, on_device(): pl.pallas_call(kernel, out_shape=(jax.ShapeDtypeStruct((16, 512), BF), ja...  95.2 us
    pallas_call x1, Pallas kernels, on_device(): pl.pallas_call(hand_over, out_shape=tuple((jax.ShapeDtypeStruct(r.shape,...  2.27 us

profile of v4, /device:TPU:1, one launch (start us, length us, event | category | flops | bytes accessed | tf_op | source)
XLA Modules:
  0.0 98.1 jit_solution(6532453278065918370)
XLA Ops:
  0.6 95.2 %shard_map.111 = (bf16[16,512]{1,0:T(8,128)(2,1)}, f32[512,256]{1,0:T(8,128)}, f32[512,256]{1,0:T(8,128)}, f32[256,512]{1,0:T(8,128)}) custom-call(bf16[16,512]{1,0:T(8,128)(2,1)} %t_ref.1, bf16[16,512]{1,0:T(8,128)(2,1)} %g_ref.1, bf16[512,256]{1,0:T(8,128)(2,1)} %wg_ref.1, bf16[512,256]{1,0:T(8,128)(2,1)} %wu_ref.1, bf16[256,512]{1,0:T(8,128)(2,1)} %wd_ref.1, ...), custom_call_target="tpu_custom_call" | custom-call | flops 1700000000 | bytes 2500000 | tf_op jit(solution)/shard_map/pallas_call | solution.py:445
  95.8 2.3 %shard_map.112 = (bf16[16,512]{1,0:T(8,128)(2,1)}, f32[512,256]{1,0:T(8,128)}, f32[512,256]{1,0:T(8,128)}, f32[256,512]{1,0:T(8,128)}) custom-call(bf16[16,512]{1,0:T(8,128)(2,1)} %get-tuple-element.8.refs_0_, f32[512,256]{1,0:T(8,128)} %get-tuple-element.9.refs_1_, f32[512,256]{1,0:T(8,128)} %get-tuple-element.10.refs_2_, f32[256,512]{1,0:T(8,128)} %get-tuple-element.11.refs_3_), custom_call_target="tpu_custom_call" | custom-call | tf_op jit(solution)/shard_map/pallas_call | solution.py:495
